TPU v7x, 512 devices: a whole 4x8x8 slice. The times are simulated.
512 devices in a mesh: shot: 32 (over y_lo, x, core), pair: 16 (over y_hi, z).
Axes of the slice: x: 4, y: 8 (y_hi: 2, y_lo: 4; y = y_hi * 4 + y_lo), z: 8, core: 2. Of those that a mesh axis runs over, the one named last changes fastest.
Arguments:
- spectra: bfloat16 [2, 512, 128, 1024], P(None, 'shot', None, 'pair'), may hold values from -6 to 6
- shot_weight: float32 [512], P('shot'), may hold values from 0.5 to 2
Outputs:
- virtual_gather: bfloat16 [2, 128, 1024, 1024], P(None, 'shot', 'pair')
All inputs are finite; a program needn't handle non-finite values.
Results may differ from a plain program's by a relative error of at most 0.0054.
Values may be sent and summed in bfloat16 or wider, within the bound.
No kernel may reach another device: no remote copies, remote signals or barrier semaphores. Data moves between devices by JAX's collectives and lax.ppermute only.
A program may use at most 64 MiB of HBM per device.

v0:
```python
import jax
import jax.numpy as jnp
from jax import lax
from jax.sharding import PartitionSpec as P


def gram_block(row_data, column_data, factor):
    swapped = jnp.stack([-row_data[1], row_data[0]])
    left_side = jnp.stack([row_data, swapped])
    product = jnp.einsum(
        "ocsfa,csfb->ofab", left_side, column_data, preferred_element_type=jnp.float32
    )
    return product * factor


def shards(spectra, shot_weight):
    scaled = (spectra.astype(jnp.float32) * shot_weight[None, :, None, None]).astype(jnp.bfloat16)
    by_freq = lax.all_to_all(scaled, "shot", split_axis=2, concat_axis=1, tiled=True)
    total_shots = by_freq.shape[1]
    factor = total_shots ** (-0.5)
    local_bins = by_freq.shape[2]
    row_width = by_freq.shape[3]
    gathered = lax.all_gather(by_freq, "pair", axis=3, tiled=True)
    device_count = lax.axis_size("pair")
    own_index = lax.axis_index("pair")

    def one_tile(tile_index):
        columns = lax.dynamic_slice_in_dim(gathered, tile_index * row_width, row_width, 3)
        return lax.cond(
            tile_index >= own_index,
            lambda: gram_block(by_freq, columns, factor).astype(jnp.bfloat16),
            lambda: jnp.zeros((2, local_bins, row_width, row_width), jnp.bfloat16),
        )

    tiles = lax.map(one_tile, jnp.arange(device_count, dtype=jnp.int32))
    received = lax.all_to_all(tiles, "pair", split_axis=0, concat_axis=0, tiled=True)
    mirrored = jnp.stack(
        [jnp.swapaxes(received[:, 0], 2, 3), -jnp.swapaxes(received[:, 1], 2, 3)], axis=1
    )
    below_diag = (jnp.arange(device_count, dtype=jnp.int32) < own_index)[:, None, None, None, None]
    merged = jnp.where(below_diag, mirrored, tiles)
    return merged.transpose(1, 2, 3, 0, 4).reshape(
        2, local_bins, row_width, device_count * row_width
    )


def solution(mesh):
    return jax.shard_map(
        shards,
        mesh=mesh,
        in_specs=(P(None, "shot", None, "pair"), P("shot")),
        out_specs=P(None, "shot", "pair", None),
        check_vma=False,
    )
```

profile of v0, /device:TPU:16, one launch (start us, length us, event | category | flops | bytes accessed | tf_op | source)
XLA Modules:
  0.0 356.7 jit_solution(6008609927738838939)
XLA Ops:
  6.5 1.2 multiply_convert_fusion
  7.8 1.6 copy.33
  9.4 0.7 reshape.12
  10.1 23.1 %all_to_all.23 = bf16[32,2,4096]{2,1,0:T(2,128)(2,1)S(1)} all-to-all(bf16[32,2,4096]{2,1,0:T(2,128)(2,1)S(1)} %reshape.12), channel_id=1, replica_groups=mesh['shot'=32,'pair'=16] {'shot'}, dimensions={0} | all-to-all | bytes 1048576 | tf_op jit(solution)/shard_map/all_to_all | solution.py:18
  34.1 1.3 copy.36
  35.8 194.2 %all-gather.2.cloned.1.call-done = bf16[2,512,4,1024]{1,2,0,3:T(4,128)(2,1)} async-done(((bf16[2,512,4,64]{1,2,0,3:T(4,128)(2,1)}), bf16[2,512,4,1024]{1,2,0,3:T(4,128)(2,1)}) %all-gather.2.cloned.1.call-update) | async-done | bytes 8388624 | tf_op jit(solution)/shard_map/all_gather | solution.py:23
  230.0 9.5 %copy.38 = bf16[2,512,4,1024]{1,3,0,2:T(8,128)(2,1)} copy(bf16[2,512,4,1024]{1,2,0,3:T(4,128)(2,1)} %all-gather.2.cloned.1.call-done) | data formatting | bytes 16777216 | tf_op jit(solution)/shard_map/while | solution.py:35
  239.5 56.6 %while.10 = (s32[]{:T(128)}, bf16[16,2,4,64,64]{4,3,1,2,0:T(8,128)(2,1)S(1)}, s32[16]{0:T(128)S(1)}, s32[]{:T(128)}, bf16[2,512,4,64]{1,3,0,2:T(8,128)(2,1)S(1)}, /*index=5*/bf16[2,512,4,1024]{1,3,0,2:T(8,128)(2,1)}, s32[]{:T(128)}) while((s32[]{:T(128)}, bf16[16,2,4,64,64]{4,3,1,2,0:T(8,128)(2,1)S(1)}, s32[16]{0:T(128)S(1)}, s32[]{:T(128)}, ...), condition=%wide.region_3.4_spmd, body=%wide.region_0.3_spmd.sunk | while | flops 68091904 | bytes 3997893 | solution.py:35
  240.7 2.2 conditional.2
  241.5 1.5 fusion.2
  244.3 2.2 conditional.2
  245.1 1.5 fusion.2
  247.8 2.2 conditional.2
  248.6 1.5 fusion.2
  251.4 2.2 conditional.2
  252.1 1.5 fusion.2
  254.9 2.2 conditional.2
  255.7 1.5 fusion.2
  258.4 2.2 conditional.2
  259.2 1.5 fusion.2
  262.0 2.2 conditional.2
  262.8 1.5 fusion.2
  265.5 2.2 conditional.2
  266.3 1.5 fusion.2
  269.1 2.2 conditional.2
  269.8 1.5 fusion.2
  272.6 2.2 conditional.2
  273.4 1.5 fusion.2
  276.1 2.2 conditional.2
  276.9 1.5 fusion.2
  279.7 2.2 conditional.2
  280.5 1.5 fusion.2
  283.2 2.2 conditional.2
  284.0 1.5 fusion.2
  286.8 2.2 conditional.2
  287.5 1.5 fusion.2
  290.3 2.2 conditional.2
  291.1 1.5 fusion.2
  293.8 2.2 conditional.2
  294.6 1.5 fusion.2
  296.1 2.6 copy.39
  298.7 4.6 %reshape.14 = bf16[16,2,16384]{2,1,0:T(2,128)(2,1)} reshape(bf16[16,2,4,64,64]{4,3,2,1,0:T(8,128)(2,1)} %bitcast.54) | data formatting | bytes 2097152
  303.4 4.5 %all-to-all-start.1 = ((bf16[16,2,16384]{2,1,0:T(2,128)(2,1)}), bf16[16,2,16384]{2,1,0:T(2,128)(2,1)}, u32[]{:S(2)}, u32[]{:S(2)}) async-start(bf16[16,2,16384]{2,1,0:T(2,128)(2,1)} %reshape.14), calls=%async_computation.1 | async-start | bytes 2097152 | tf_op jit(solution)/shard_map/all_to_all | solution.py:36
  307.9 31.3 %all-to-all-done.1 = bf16[16,2,16384]{2,1,0:T(2,128)(2,1)} async-done(((bf16[16,2,16384]{2,1,0:T(2,128)(2,1)}), bf16[16,2,16384]{2,1,0:T(2,128)(2,1)}, u32[]{:S(2)}, u32[]{:S(2)}) %all-to-all-start.1) | async-done | bytes 1048608 | tf_op jit(solution)/shard_map/all_to_all | solution.py:36
  339.2 4.7 %reshape.15 = bf16[16,2,4,64,64]{4,3,2,1,0:T(8,128)(2,1)} reshape(bf16[16,2,16384]{2,1,0:T(2,128)(2,1)} %all-to-all-done.1) | data formatting | bytes 2097152
  343.9 1.7 slice_bitcast_fusion
  346.2 1.4 copy.42
  347.6 2.3 reshape.9
  (75 shorter events, 13.0 us)
Async XLA Ops:
  6.5 223.5 %all-gather.2.cloned.1.call-start = ((), (), s32[]{:S(2)}) async-start(), calls=%async_computation.2 | async-start | bytes 8912896 | tf_op jit(solution)/shard_map/all_gather | solution.py:23
  35.8 203.7 %copy-start = (bf16[16,2,4,64,64]{4,3,1,2,0:T(8,128)(2,1)S(1)}, bf16[16,2,4,64,64]{4,3,1,2,0:T(8,128)(2,1)}, u32[]{:S(2)}) copy-start(bf16[16,2,4,64,64]{4,3,1,2,0:T(8,128)(2,1)} %custom-call) | copy-start | bytes 3145732
  303.4 35.8 %all-to-all-start.1 = ((bf16[16,2,16384]{2,1,0:T(2,128)(2,1)}), bf16[16,2,16384]{2,1,0:T(2,128)(2,1)}, u32[]{:S(2)}, u32[]{:S(2)}) async-start(bf16[16,2,16384]{2,1,0:T(2,128)(2,1)} %reshape.14), calls=%async_computation.1 | async-start | bytes 2097152 | tf_op jit(solution)/shard_map/all_to_all | solution.py:36
Sparse Core Ops, SparseCore 0:
  35.6 194.4 all-gather.1
where the time goes:
time: 358 us; the launch traced here: 357 us
  waiting for transfers between devices  226 us (63%)
  local copies, waits for them, and re-layouts  39.7 us (11%)
  matrix products  23.5 us (7%)
  blocking collectives  23.1 us (6%)
  loops' own time  21.9 us (6%)
  between operations  13.5 us (4%)
  other arithmetic  4.96 us (1%)
  starting transfers between devices  4.54 us (1%)
    all_gather x1, waiting for transfers between devices, shards(): gathered = lax.all_gather(by_freq, 'pair', axis=3, tiled=True)  194 us
    all_to_all x1, waiting for transfers between devices, shards(): lax.all_to_all(tiles, 'pair', split_axis=0, concat_axis=0, tiled=True)  31.3 us
    dot_general x16, matrix products, gram_block(): jnp.einsum('ocsfa,csfb->ofab', left_side, column_data, preferred_element_...  23.5 us
    all_to_all x1, blocking collectives, shards(): lax.all_to_all(scaled, 'shot', split_axis=2, concat_axis=1, tiled=True)  23.1 us
    while x3, local copies, waits for them, and re-layouts, shards(): tiles = lax.map(one_tile, jnp.arange(device_count, dtype=jnp.int32))  12.4 us
    another operation x16, loops' own time, one_tile(): lax.cond(tile_index >= own_index, lambda: gram_block(by_freq, columns, fa...  11 us
    another operation x1, loops' own time, shards(): tiles = lax.map(one_tile, jnp.arange(device_count, dtype=jnp.int32))  10.9 us
    unnamed x6, local copies, waits for them, and re-layouts  10.7 us
  transfers between devices with their start and end apart: 2, of which 2 were waited for; matrix products, arithmetic and copies ran while one was open for 0% of the time, Pallas kernels for 0%

commit v1 on v0

--- a/solution.py
+++ b/solution.py
@@ -20,7 +20,9 @@
     factor = total_shots ** (-0.5)
     local_bins = by_freq.shape[2]
     row_width = by_freq.shape[3]
-    gathered = lax.all_gather(by_freq, "pair", axis=3, tiled=True)
+    gathered = jnp.concatenate(
+        lax.all_to_all(jnp.stack([by_freq] * lax.axis_size("pair")), "pair", 0, 0), axis=3
+    )
     device_count = lax.axis_size("pair")
     own_index = lax.axis_index("pair")
 

time: 358 us -> 495 us (1.38)
  the two profiles are of different devices: /device:TPU:16 before, /device:TPU:112 now
where the time goes in v1:
time: 495 us; the launch traced here: 494 us
  waiting for transfers between devices  349 us (71%)
  local copies, waits for them, and re-layouts  46.4 us (9%)
  starting transfers between devices  46.3 us (9%)
  blocking collectives  21.5 us (4%)
  loops' own time  15.5 us (3%)
  matrix products  10.3 us (2%)
    all_to_all x1, waiting for transfers between devices, shards(): lax.all_to_all(jnp.stack([by_freq] * lax.axis_size('pair')), 'pair', 0, 0)  322 us
    all_to_all x1, starting transfers between devices, shards(): lax.all_to_all(tiles, 'pair', split_axis=0, concat_axis=0, tiled=True)  31.5 us
    all_to_all x1, waiting for transfers between devices, shards(): lax.all_to_all(tiles, 'pair', split_axis=0, concat_axis=0, tiled=True)  26.8 us
    all_to_all x1, blocking collectives, shards(): lax.all_to_all(scaled, 'shot', split_axis=2, concat_axis=1, tiled=True)  21.5 us
    all_to_all x1, starting transfers between devices, shards(): lax.all_to_all(jnp.stack([by_freq] * lax.axis_size('pair')), 'pair', 0, 0)  14.8 us
    another operation x1, loops' own time, shards(): tiles = lax.map(one_tile, jnp.arange(device_count, dtype=jnp.int32))  10.7 us
    dot_general x7, matrix products, gram_block(): jnp.einsum('ocsfa,csfb->ofab', left_side, column_data, preferred_element_...  10.3 us
    while x3, local copies, waits for them, and re-layouts, shards(): tiles = lax.map(one_tile, jnp.arange(device_count, dtype=jnp.int32))  10.1 us
  transfers between devices with their start and end apart: 2, of which 2 were waited for; matrix products, arithmetic and copies ran while one was open for 0% of the time, Pallas kernels for 0%

profile of v1, /device:TPU:112, one launch (start us, length us, event | category | flops | bytes accessed | tf_op | source)
XLA Modules:
  0.0 493.5 jit_solution(3526894565201540518)
XLA Ops:
  0.0 1.2 multiply_convert_fusion
  1.2 1.6 copy.33
  2.8 0.7 reshape.23
  3.6 21.5 %all_to_all.25 = bf16[32,2,4096]{2,1,0:T(2,128)(2,1)S(1)} all-to-all(bf16[32,2,4096]{2,1,0:T(2,128)(2,1)S(1)} %reshape.23), channel_id=1, replica_groups=mesh['shot'=32,'pair'=16] {'shot'}, dimensions={0} | all-to-all | bytes 1048576 | tf_op jit(solution)/shard_map/all_to_all | solution.py:18
  25.1 0.7 reshape.24
  26.3 4.3 stack.52
  30.6 14.8 %all-to-all-start.1 = ((bf16[16,2,512,4,64]{2,4,1,3,0:T(8,128)(2,1)}), bf16[16,2,512,4,64]{2,4,1,3,0:T(8,128)(2,1)}, u32[]{:S(2)}, u32[]{:S(2)}) async-start(bf16[16,2,512,4,64]{2,4,1,3,0:T(8,128)(2,1)} %stack.52), calls=%async_computation.1 | async-start | bytes 16777216 | tf_op jit(solution)/shard_map/all_to_all | solution.py:24
  45.4 322.4 %all-to-all-done.1 = bf16[16,2,512,4,64]{2,4,1,3,0:T(8,128)(2,1)} async-done(((bf16[16,2,512,4,64]{2,4,1,3,0:T(8,128)(2,1)}), bf16[16,2,512,4,64]{2,4,1,3,0:T(8,128)(2,1)}, u32[]{:S(2)}, u32[]{:S(2)}) %all-to-all-start.1) | async-done | bytes 8388640 | tf_op jit(solution)/shard_map/all_to_all | solution.py:24
  367.8 7.7 %copy.37 = bf16[16,2,512,4,64]{2,4,0,3,1:T(8,128)(2,1)} copy(bf16[16,2,512,4,64]{2,4,1,3,0:T(8,128)(2,1)} %all-to-all-done.1) | data formatting | bytes 16777216 | tf_op jit(solution)/shard_map/all_to_all | solution.py:24
  375.5 7.2 %copy.39 = bf16[2,512,4,1024]{1,3,0,2:T(8,128)(2,1)} copy(bf16[2,512,4,1024]{1,3,2,0:T(8,128)(2,1)} %bitcast.53) | data formatting | bytes 16777216 | tf_op jit(solution)/shard_map/while | solution.py:37
  382.6 36.9 %while.10 = (s32[]{:T(128)}, bf16[16,2,4,64,64]{4,3,1,2,0:T(8,128)(2,1)S(1)}, s32[16]{0:T(128)S(1)}, s32[]{:T(128)}, bf16[2,512,4,64]{1,3,0,2:T(8,128)(2,1)S(1)}, /*index=5*/bf16[2,512,4,1024]{1,3,0,2:T(8,128)(2,1)}, s32[]{:T(128)}) while((s32[]{:T(128)}, bf16[16,2,4,64,64]{4,3,1,2,0:T(8,128)(2,1)S(1)}, s32[16]{0:T(128)S(1)}, s32[]{:T(128)}, ...), condition=%wide.region_3.4_spmd, body=%wide.region_0.3_spmd.sunk | while | flops 68091904 | bytes 3997885 | solution.py:37
  384.0 0.6 dynamic_slice.17
  385.3 0.6 dynamic_slice.17
  386.7 0.6 dynamic_slice.17
  388.0 0.6 dynamic_slice.17
  389.4 0.6 dynamic_slice.17
  390.7 0.6 dynamic_slice.17
  392.1 0.6 dynamic_slice.17
  393.4 0.6 dynamic_slice.17
  394.8 0.6 dynamic_slice.17
  396.1 2.2 conditional.2
  396.8 1.5 fusion.2
  398.3 0.6 dynamic_slice.17
  399.6 2.2 conditional.2
  400.4 1.5 fusion.2
  401.9 0.6 dynamic_slice.17
  403.1 2.2 conditional.2
  403.9 1.5 fusion.2
  405.4 0.6 dynamic_slice.17
  406.7 2.2 conditional.2
  407.4 1.5 fusion.2
  408.9 0.6 dynamic_slice.17
  410.2 2.2 conditional.2
  411.0 1.5 fusion.2
  412.5 0.6 dynamic_slice.17
  413.7 2.2 conditional.2
  414.5 1.5 fusion.2
  416.0 0.6 dynamic_slice.17
  417.3 2.2 conditional.2
  418.0 1.5 fusion.2
  419.6 2.6 copy.40
  422.2 4.6 reshape.25
  426.8 31.5 %all-to-all-start.2 = ((bf16[16,2,16384]{2,1,0:T(2,128)(2,1)}), bf16[16,2,16384]{2,1,0:T(2,128)(2,1)S(1)}, u32[]{:S(2)}, u32[]{:S(2)}) async-start(bf16[16,2,16384]{2,1,0:T(2,128)(2,1)} %reshape.25), calls=%async_computation.2 | async-start | bytes 2097152 | tf_op jit(solution)/shard_map/all_to_all | solution.py:38
  458.4 26.8 %all-to-all-done.2 = bf16[16,2,16384]{2,1,0:T(2,128)(2,1)S(1)} async-done(((bf16[16,2,16384]{2,1,0:T(2,128)(2,1)}), bf16[16,2,16384]{2,1,0:T(2,128)(2,1)S(1)}, u32[]{:S(2)}, u32[]{:S(2)}) %all-to-all-start.2) | async-done | bytes 1048608 | tf_op jit(solution)/shard_map/all_to_all | solution.py:38
  485.2 2.4 reshape.26
  487.5 1.7 slice_bitcast_fusion
  489.9 1.4 copy.43
  491.2 2.3 reshape.20
  (55 shorter events, 3.3 us)
Async XLA Ops:
  30.6 337.2 %all-to-all-start.1 = ((bf16[16,2,512,4,64]{2,4,1,3,0:T(8,128)(2,1)}), bf16[16,2,512,4,64]{2,4,1,3,0:T(8,128)(2,1)}, u32[]{:S(2)}, u32[]{:S(2)}) async-start(bf16[16,2,512,4,64]{2,4,1,3,0:T(8,128)(2,1)} %stack.52), calls=%async_computation.1 | async-start | bytes 16777216 | tf_op jit(solution)/shard_map/all_to_all | solution.py:24
  426.8 58.4 %all-to-all-start.2 = ((bf16[16,2,16384]{2,1,0:T(2,128)(2,1)}), bf16[16,2,16384]{2,1,0:T(2,128)(2,1)S(1)}, u32[]{:S(2)}, u32[]{:S(2)}) async-start(bf16[16,2,16384]{2,1,0:T(2,128)(2,1)} %reshape.25), calls=%async_computation.2 | async-start | bytes 2097152 | tf_op jit(solution)/shard_map/all_to_all | solution.py:38
